TPU v7x, 32 devices: a whole 2x2x4 slice. The times are simulated.
32 devices in a mesh: mesh: 8 (over z, x), freq: 4 (over y, core).
Axes of the slice: x: 2, y: 2, z: 4, core: 2. Of those that a mesh axis runs over, the one named last changes fastest.
Arguments:
- spectra: float32 [36, 36, 4096], P('freq', None, 'mesh'), may hold values from 0.1 to 2
- coords: float32 [2, 4096], P(None, 'mesh'), may hold values from -5 to 5
- inv_area: float32 [4096], P('mesh'), may hold values from 0.3 to 1
- wind_vector: float32 [2, 4096], P(None, 'mesh'), may hold values from -6 to 6
- neighbours: int32 [8, 4096], P(None, 'mesh'), may hold values from 0 to 767, as said below
- send_nodes: int32 [64, 32], P('mesh'), may hold values from 0 to 511
- send_count: int32 [64], P('mesh'), may hold values from 1 to 32, as said below
Outputs:
- updated: float32 [36, 36, 4096], P('freq', None, 'mesh')
Inputs may be any that keep to these rules, and one draw needn't show every extreme that they name: `neighbours`: an entry below 512 is a node of the same partition; an entry 512 + q * 32 + c names slot c of the list that partition q sends to this partition, with c below that list's count; slots past a node's degree name the node itself; some node uses all 8 slots. `send_count`: in every draw some partition receives exactly 32 nodes from every partition.
All inputs are finite; a program needn't handle non-finite values.
Results may differ from a plain program's by a relative error of at most 0.00002.
Values sent between devices are 32-bit elements; how exact they have to be, the bound alone decides.
A program may use at most 64 MiB of HBM per device.

v0:
```python
import functools
import math

import jax
import jax.numpy as jnp
from jax import lax
from jax.experimental import pallas as pl
from jax.experimental.pallas import tpu as pltpu
from jax.sharding import PartitionSpec as P

NF = 36
REACH = 3
UP_REACH = REACH - 1
UP_SHIFT = 1
DOWN_SHIFT = 3

time_step = 0.5
group_scale = 0.8
quad_coupling = 0.25
wind_growth = 0.1
freq_ratio = 1.1

MESH = pl.DeviceIdType.MESH
ROWS = 128
SPARE = 120
PER = 3
PITCH = 40


def split2(x):
    hi = x.astype(jnp.bfloat16)
    lo = (x - hi.astype(jnp.float32)).astype(jnp.bfloat16)
    return hi, lo


def roll_rows(x, shift):
    count = x.shape[0]
    cut = (-shift) % count
    return jnp.concatenate([x[cut:], x[:cut]], axis=0)


def kernel(
    n_mesh, n_freq, dirs, cap,
    spec_ref, coords_ref, inv_ref, wind_ref, nb_ref, send_ref, count_ref,
    out_ref,
    cur, lhs, picked, base, acc, weights, wsum, hot, hot_send, pay, recv, halo_lo, halo_hi,
    send_sem, recv_sem, halo_sem,
):
    band = spec_ref.shape[0]
    nodes = spec_ref.shape[2]
    slots = nb_ref.shape[0]
    ghosts = n_mesh * cap
    chunks = band // PER
    f32 = jnp.float32
    bf16 = jnp.bfloat16
    me = lax.axis_index("mesh")
    fi = lax.axis_index("freq")

    barrier = pltpu.get_barrier_semaphore()
    for off in range(1, n_mesh):
        pl.semaphore_signal(
            barrier, inc=1, device_id={"mesh": lax.rem(me + off, n_mesh)}, device_id_type=MESH
        )

    @pl.when(fi > 0)
    def _():
        pl.semaphore_signal(barrier, inc=1, device_id={"freq": fi - 1}, device_id_type=MESH)

    @pl.when(fi < n_freq - 1)
    def _():
        pl.semaphore_signal(barrier, inc=1, device_id={"freq": fi + 1}, device_id_type=MESH)

    cells = send_ref[...].astype(f32)
    lane_c = lax.broadcasted_iota(jnp.int32, (cap, ghosts), 1) % cap
    spread = (lane_c == lax.broadcasted_iota(jnp.int32, (cap, ghosts), 0)).astype(f32)
    wide = jnp.dot(cells, spread, precision=lax.Precision.HIGHEST, preferred_element_type=f32)
    owner_lane = lax.broadcasted_iota(jnp.int32, (n_mesh, ghosts), 1) // cap
    mine = owner_lane == lax.broadcasted_iota(jnp.int32, (n_mesh, ghosts), 0)
    send_row = jnp.sum(jnp.where(mine, wide, 0.0), axis=0, keepdims=True)
    send_row = (send_row + 0.5).astype(jnp.int32)
    lane = lax.broadcasted_iota(jnp.int32, (1, ghosts), 1)
    limit = jnp.zeros((1, ghosts), jnp.int32)
    for d in range(n_mesh):
        limit = jnp.where(lane // cap == d, count_ref[d], limit)
    send_row = jnp.where(lane % cap < limit, send_row, -1)
    hot_send[...] = (
        (lax.broadcasted_iota(jnp.int32, (nodes, ghosts), 0) == send_row).astype(f32).astype(bf16)
    )

    for c in range(chunks):
        cur[c] = jnp.zeros((ROWS, nodes), f32)
        for j in range(PER):
            cur[c, j * PITCH : j * PITCH + dirs, :] = spec_ref[c * PER + j]
    x_own = coords_ref[0:1, :]
    y_own = coords_ref[1:2, :]
    cur[0, SPARE : SPARE + 1, :] = x_own
    cur[0, SPARE + 1 : SPARE + 2, :] = y_own
    for r, row in ((2, x_own), (3, y_own)):
        hi, lo = split2(row)
        rest = (row - hi.astype(f32)) - lo.astype(f32)
        cur[0, SPARE + r : SPARE + r + 1, :] = rest

    def copy_of(stage, off, src_rank, dst_rank, target):
        return pltpu.make_async_remote_copy(
            src_ref=pay.at[stage, pl.ds(pl.multiple_of(src_rank * cap, cap), cap), :],
            dst_ref=recv.at[stage, pl.ds(pl.multiple_of(dst_rank * cap, cap), cap), :],
            send_sem=send_sem.at[stage, off],
            recv_sem=recv_sem.at[stage, off],
            device_id={"mesh": target},
            device_id_type=MESH,
        )

    def pack(stage, c):
        both = jnp.dot(lhs[c], hot_send[...], preferred_element_type=f32)
        pay[stage] = jnp.transpose(both[:ROWS] + both[ROWS:])

    def send(stage):
        for off in range(1, n_mesh):
            to = lax.rem(me + off, n_mesh)
            copy_of(stage, off, to, me, to).start()

    def own(stage):
        at = pl.ds(pl.multiple_of(me * cap, cap), cap)
        recv[stage, at, :] = pay[stage, at, :]

    def arrive(stage):
        for off in range(1, n_mesh):
            copy_of(stage, off, 0, me, lax.rem(me + off, n_mesh)).wait_recv()

    def ghosts_of(stage):
        hi, lo = split2(jnp.transpose(recv[stage]))
        return jnp.concatenate([hi, lo], axis=0)

    def split_chunk(c):
        hi, lo = split2(cur[c])
        lhs[c, 0:ROWS] = hi
        lhs[c, ROWS : 2 * ROWS] = lo

    for c in range(chunks):
        split_chunk(c)
        pack(c, c)

    expected = (n_mesh - 1) + (fi > 0).astype(jnp.int32) + (fi < n_freq - 1).astype(jnp.int32)
    pl.semaphore_wait(barrier, expected)
    for c in range(chunks):
        send(c)

    up_copy = pltpu.make_async_remote_copy(
        src_ref=spec_ref.at[pl.ds(band - REACH, REACH)], dst_ref=halo_lo,
        send_sem=halo_sem.at[0], recv_sem=halo_sem.at[1],
        device_id={"freq": lax.rem(fi + 1, n_freq)}, device_id_type=MESH,
    )
    down_copy = pltpu.make_async_remote_copy(
        src_ref=spec_ref.at[pl.ds(0, UP_REACH)], dst_ref=halo_hi,
        send_sem=halo_sem.at[2], recv_sem=halo_sem.at[3],
        device_id={"freq": lax.rem(fi + n_freq - 1, n_freq)}, device_id_type=MESH,
    )

    @pl.when(fi < n_freq - 1)
    def _():
        up_copy.start()

    @pl.when(fi > 0)
    def _():
        down_copy.start()

    @pl.when(fi == 0)
    def _():
        halo_lo[...] = jnp.zeros(halo_lo.shape, f32)

    @pl.when(fi == n_freq - 1)
    def _():
        halo_hi[...] = jnp.zeros(halo_hi.shape, f32)

    for c in range(chunks):
        own(c)

    def build(k, carry):
        entry = nb_ref[pl.ds(k, 1), :]
        rows = lax.broadcasted_iota(jnp.int32, (nodes + ghosts, nodes), 0)
        hot[k] = (rows == entry).astype(f32).astype(bf16)
        for c in range(chunks):
            both = jnp.dot(lhs[c], hot[k, 0:nodes], preferred_element_type=f32)
            picked[k, c] = both[:ROWS] + both[ROWS:]
        return carry

    lax.fori_loop(0, slots, build, 0)

    angle = (lax.broadcasted_iota(jnp.int32, (PITCH, 128), 0).astype(f32) + 0.5) * (
        2.0 * math.pi / dirs
    )
    real = lax.broadcasted_iota(jnp.int32, (PITCH, 128), 0) < dirs
    cosine = jnp.where(real, jnp.cos(angle), 0.0)[:, 0:1]
    sine = jnp.where(real, jnp.sin(angle), 0.0)[:, 0:1]
    ratios = []
    for j in range(band):
        value = jnp.float32(freq_ratio ** (j - NF // 2))
        for b in range(1, n_freq):
            value = jnp.where(fi == b, jnp.float32(freq_ratio ** (b * band + j - NF // 2)), value)
        ratios.append(value)

    @pl.when(fi > 0)
    def _():
        up_copy.wait_recv()

    @pl.when(fi < n_freq - 1)
    def _():
        down_copy.wait_recv()

    along = cosine[:dirs] * wind_ref[0:1, :] + sine[:dirs] * wind_ref[1:2, :]
    for j in range(band):
        own_bin = spec_ref[j]
        upper = spec_ref[j + UP_REACH] if j + UP_REACH < band else halo_hi[j + UP_REACH - band]
        lower = spec_ref[j - REACH] if j >= REACH else halo_lo[j]
        p1 = roll_rows(upper, -UP_SHIFT)
        m1 = roll_rows(lower, DOWN_SHIFT)
        p2 = roll_rows(upper, UP_SHIFT)
        m2 = roll_rows(lower, -DOWN_SHIFT)
        quad = quad_coupling * (
            own_bin * own_bin * (p1 + m1 + p2 + m2) - 2.0 * own_bin * (p1 * m1 + p2 * m2)
        )
        growth = wind_growth * jnp.maximum(along * ratios[j] - 1.0, 0.0)
        c, at = j // PER, (j % PER) * PITCH
        base[c, at : at + dirs, :] = own_bin + time_step * (quad + growth * own_bin)
        base[c, at + dirs : at + PITCH, :] = jnp.zeros((PITCH - dirs, nodes), f32)

    speeds = [group_scale / r for r in ratios]
    scale = time_step * inv_ref[...]

    def finish(c, j, store):
        at = j * PITCH
        speed = speeds[c * PER + j]
        store(
            (base[c, at : at + PITCH, :] + speed * acc[c, at : at + PITCH, :])
            / (1.0 + speed * wsum[...])
        )

    wsum[...] = jnp.zeros(wsum.shape, f32)

    for c in range(chunks):
        arrive(c)
        far = ghosts_of(c)
        acc[c] = jnp.zeros((SPARE, nodes), f32)

        def slot1(k, carry, c=c, far=far):
            both = jnp.dot(far, hot[k, nodes:], preferred_element_type=f32)
            value = picked[k, c] + (both[:ROWS] + both[ROWS:])
            if c == 0:
                dx = (value[SPARE : SPARE + 1] + value[SPARE + 2 : SPARE + 3]) - x_own
                dy = (value[SPARE + 1 : SPARE + 2] + value[SPARE + 3 : SPARE + 4]) - y_own
                w = scale * jnp.maximum(-(cosine * dx + sine * dy), 0.0)
                weights[k] = w
                wsum[...] += w
            else:
                w = weights[k]
            for j in range(PER):
                at = j * PITCH
                acc[c, at : at + PITCH, :] += w * value[at : at + PITCH]
            return carry

        lax.fori_loop(0, slots, slot1, 0)
        for j in range(PER):
            def store(v, c=c, at=j * PITCH):
                cur[c, at : at + PITCH, :] = v

            finish(c, j, store)
        split_chunk(c)
        pack(chunks + c, c)
        send(chunks + c)
        own(chunks + c)
        acc[c] = jnp.zeros((SPARE, nodes), f32)

        def local2(k, carry, c=c):
            both = jnp.dot(lhs[c], hot[k, 0:nodes], preferred_element_type=f32)
            w = weights[k]
            for j in range(PER):
                at = j * PITCH
                acc[c, at : at + PITCH, :] += w * (
                    both[at : at + PITCH] + both[ROWS + at : ROWS + at + PITCH]
                )
            return carry

        lax.fori_loop(0, slots, local2, 0)

    for c in range(chunks):
        arrive(chunks + c)
        far = ghosts_of(chunks + c)

        def slot2(k, carry, c=c, far=far):
            both = jnp.dot(far, hot[k, nodes:], preferred_element_type=f32)
            w = weights[k]
            for j in range(PER):
                at = j * PITCH
                acc[c, at : at + PITCH, :] += w * (
                    both[at : at + PITCH] + both[ROWS + at : ROWS + at + PITCH]
                )
            return carry

        lax.fori_loop(0, slots, slot2, 0)
        for j in range(PER):
            def store(v, f=c * PER + j):
                out_ref[f] = v[:dirs]

            finish(c, j, store)

    for stage in range(2 * chunks):
        for off in range(1, n_mesh):
            to = lax.rem(me + off, n_mesh)
            copy_of(stage, off, to, me, to).wait_send()

    @pl.when(fi < n_freq - 1)
    def _():
        up_copy.wait_send()

    @pl.when(fi > 0)
    def _():
        down_copy.wait_send()


def local(n_mesh, n_freq, spectra, coords, inv_area, wind_vector, neighbours, send_nodes, send_count):
    band, dirs, nodes = spectra.shape
    cap = send_nodes.shape[1]
    slots = neighbours.shape[0]
    ghosts = n_mesh * cap
    chunks = band // PER
    f32, bf16 = jnp.float32, jnp.bfloat16
    vmem = pl.BlockSpec(memory_space=pltpu.VMEM)
    return pl.pallas_call(
        functools.partial(kernel, n_mesh, n_freq, dirs, cap),
        out_shape=jax.ShapeDtypeStruct(spectra.shape, f32),
        in_specs=[vmem] * 6 + [pl.BlockSpec(memory_space=pltpu.SMEM)],
        out_specs=vmem,
        scratch_shapes=[
            pltpu.VMEM((chunks, ROWS, nodes), f32),
            pltpu.VMEM((chunks, 2 * ROWS, nodes), bf16),
            pltpu.VMEM((slots, chunks, ROWS, nodes), f32),
            pltpu.VMEM((chunks, SPARE, nodes), f32),
            pltpu.VMEM((chunks, SPARE, nodes), f32),
            pltpu.VMEM((slots, PITCH, nodes), f32),
            pltpu.VMEM((PITCH, nodes), f32),
            pltpu.VMEM((slots, nodes + ghosts, nodes), bf16),
            pltpu.VMEM((nodes, ghosts), bf16),
            pltpu.VMEM((2 * chunks, ghosts, ROWS), f32),
            pltpu.VMEM((2 * chunks, ghosts, ROWS), f32),
            pltpu.VMEM((REACH, dirs, nodes), f32),
            pltpu.VMEM((UP_REACH, dirs, nodes), f32),
            pltpu.SemaphoreType.DMA((2 * chunks, n_mesh)),
            pltpu.SemaphoreType.DMA((2 * chunks, n_mesh)),
            pltpu.SemaphoreType.DMA((4,)),
        ],
        compiler_params=pltpu.CompilerParams(
            collective_id=0, has_side_effects=True, vmem_limit_bytes=48 * 1024 * 1024
        ),
        cost_estimate=pl.CostEstimate(
            flops=4 * 2 * band * dirs * (nodes + ghosts) * nodes * slots,
            bytes_accessed=2 * 4 * band * dirs * nodes,
            transcendentals=0,
        ),
    )(spectra, coords, inv_area.reshape(1, nodes), wind_vector, neighbours, send_nodes, send_count)


def solution(mesh):
    in_specs = (
        P("freq", None, "mesh"),
        P(None, "mesh"),
        P("mesh"),
        P(None, "mesh"),
        P(None, "mesh"),
        P("mesh", None),
        P("mesh"),
    )
    return jax.shard_map(
        functools.partial(local, mesh.shape["mesh"], mesh.shape["freq"]),
        mesh=mesh, in_specs=in_specs, out_specs=P("freq", None, "mesh"), check_vma=False,
    )
```

profile of v0, /device:TPU:0, one launch (start us, length us, event | category | flops | bytes accessed | tf_op | source)
XLA Modules:
  0.0 41.3 jit_solution(1267197432357618219)
XLA Ops:
  0.0 0.0 copy-start.6
  0.0 0.7 %copy-done.6 = s32[8]{0:T(128)S(1)} copy-done((s32[8]{0:T(128)S(1)}, s32[8]{0:T(128)}, u32[]{:S(2)}) %copy-start.6) | copy-done | bytes 56
  0.7 0.0 copy-start
  0.7 1.1 %copy-done = f32[9,36,512]{2,1,0:T(8,128)S(1)} copy-done((f32[9,36,512]{2,1,0:T(8,128)S(1)}, f32[9,36,512]{2,1,0:T(8,128)}, u32[]{:S(2)}) %copy-start) | copy-done | bytes 663576
  1.8 0.0 copy-start.1
  1.8 0.7 %copy-done.1 = s32[8,512]{1,0:T(8,128)S(1)} copy-done((s32[8,512]{1,0:T(8,128)S(1)}, s32[8,512]{1,0:T(8,128)}, u32[]{:S(2)}) %copy-start.1) | copy-done | bytes 16408
  2.5 0.0 copy-start.2
  2.5 0.7 %copy-done.2 = f32[2,512]{1,0:T(2,128)S(1)} copy-done((f32[2,512]{1,0:T(2,128)S(1)}, f32[2,512]{1,0:T(2,128)}, u32[]{:S(2)}) %copy-start.2) | copy-done | bytes 4120
  3.2 0.0 copy-start.3
  3.2 0.7 %copy-done.3 = f32[2,512]{1,0:T(2,128)S(1)} copy-done((f32[2,512]{1,0:T(2,128)S(1)}, f32[2,512]{1,0:T(2,128)}, u32[]{:S(2)}) %copy-start.3) | copy-done | bytes 4120
  3.9 0.0 copy-start.4
  3.9 0.7 %copy-done.4 = s32[8,32]{1,0:T(8,128)S(1)} copy-done((s32[8,32]{1,0:T(8,128)S(1)}, s32[8,32]{1,0:T(8,128)}, u32[]{:S(2)}) %copy-start.4) | copy-done | bytes 1048
  4.6 0.0 copy-start.5
  4.6 0.7 %copy-done.5 = f32[512]{0:T(512)S(1)} copy-done((f32[512]{0:T(512)S(1)}, f32[512]{0:T(512)}, u32[]{:S(2)}) %copy-start.5) | copy-done | bytes 2072
  5.2 35.2 %shard_map.73 = f32[9,36,512]{2,1,0:T(8,128)S(1)} custom-call(f32[9,36,512]{2,1,0:T(8,128)S(1)} %copy-done, f32[2,512]{1,0:T(2,128)S(1)} %copy-done.2, f32[1,512]{1,0:T(1,128)S(1)} %bitcast.1, f32[2,512]{1,0:T(2,128)S(1)} %copy-done.3, s32[8,512]{1,0:T(8,128)S(1)} %copy-done.1, s32[8,32]{1,0:T(8,128)S(1)} %copy-done.4, s32[8]{0:T(128)S(1)} %copy-done.6), custom_call_target="tpu_custom_call" | custom-call | flops 8153726976 | bytes 1327104 | tf_op jit(solution)/shard_map/pallas_call | solution.py:328
  40.5 0.9 %copy.9 = f32[9,36,512]{2,1,0:T(8,128)} copy(f32[9,36,512]{2,1,0:T(8,128)S(1)} %shard_map.73) | data formatting | bytes 1327104
Async XLA Ops:
  0.0 0.7 %copy-start.6 = (s32[8]{0:T(128)S(1)}, s32[8]{0:T(128)}, u32[]{:S(2)}) copy-start(s32[8]{0:T(128)} %count_ref.1) | copy-start | bytes 100
  0.7 1.1 %copy-start = (f32[9,36,512]{2,1,0:T(8,128)S(1)}, f32[9,36,512]{2,1,0:T(8,128)}, u32[]{:S(2)}) copy-start(f32[9,36,512]{2,1,0:T(8,128)} %spec_ref.1) | copy-start | bytes 1990660
  1.8 0.7 %copy-start.1 = (s32[8,512]{1,0:T(8,128)S(1)}, s32[8,512]{1,0:T(8,128)}, u32[]{:S(2)}) copy-start(s32[8,512]{1,0:T(8,128)} %nb_ref.1) | copy-start | bytes 49156
  2.5 0.7 %copy-start.2 = (f32[2,512]{1,0:T(2,128)S(1)}, f32[2,512]{1,0:T(2,128)}, u32[]{:S(2)}) copy-start(f32[2,512]{1,0:T(2,128)} %coords_ref.1) | copy-start | bytes 12292
  3.2 0.7 %copy-start.3 = (f32[2,512]{1,0:T(2,128)S(1)}, f32[2,512]{1,0:T(2,128)}, u32[]{:S(2)}) copy-start(f32[2,512]{1,0:T(2,128)} %wind_ref.1) | copy-start | bytes 12292
  3.9 0.7 %copy-start.4 = (s32[8,32]{1,0:T(8,128)S(1)}, s32[8,32]{1,0:T(8,128)}, u32[]{:S(2)}) copy-start(s32[8,32]{1,0:T(8,128)} %send_ref.1) | copy-start | bytes 3076
  4.6 0.7 %copy-start.5 = (f32[512]{0:T(512)S(1)}, f32[512]{0:T(512)}, u32[]{:S(2)}) copy-start(f32[512]{0:T(512)} %param.9) | copy-start | bytes 6148
where the time goes:
time: 41.7 us; the launch traced here: 41.3 us
  Pallas kernels  35.2 us (84%)
  local copies, waits for them, and re-layouts  6.09 us (15%)
    pallas_call x1, Pallas kernels, local(): pl.pallas_call(functools.partial(kernel, n_mesh, n_freq, dirs, cap), out_...  35.2 us
    unnamed x15, local copies, waits for them, and re-layouts  6.09 us

commit v1 on v0

v1 whole, which is shorter than its diff:
```python
import functools
import math

import jax
import jax.numpy as jnp
from jax import lax
from jax.experimental import pallas as pl
from jax.experimental.pallas import tpu as pltpu
from jax.sharding import PartitionSpec as P

NF = 36
REACH = 3
UP_REACH = REACH - 1
UP_SHIFT = 1
DOWN_SHIFT = 3

time_step = 0.5
group_scale = 0.8
quad_coupling = 0.25
wind_growth = 0.1
freq_ratio = 1.1

MESH = pl.DeviceIdType.MESH
PER = 3
LANES = 128


def split2(x):
    hi = x.astype(jnp.bfloat16)
    lo = (x - hi.astype(jnp.float32)).astype(jnp.bfloat16)
    return hi, lo


def roll_rows(x, shift):
    count = x.shape[0]
    cut = (-shift) % count
    return jnp.concatenate([x[cut:], x[:cut]], axis=0)


def kernel(
    n_mesh, n_freq, dirs, cap,
    spec_hbm, coords_hbm, inv_hbm, wind_hbm, nb_hbm, send_hbm, count_hbm,
    out_ref,
    spec_ref, coords_ref, inv_ref, wind_ref, nb_ref, send_ref, count_ref,
    lhs, picked, base, acc, weights, hot, hot_send, pay, recv, halo_lo, halo_hi,
    in_sem, send_sem, recv_sem, halo_sem,
):
    band = spec_ref.shape[0]
    nodes = spec_ref.shape[2]
    slots = nb_ref.shape[0]
    ghosts = n_mesh * cap
    chunks = band // PER
    main = dirs // 8 * 8
    rest = dirs - main
    rows = lhs.shape[1] // 2
    tail = PER * main
    spare = tail + PER * rest
    tail_rows = rows - tail
    half = nodes // 2
    f32 = jnp.float32
    bf16 = jnp.bfloat16
    me = lax.axis_index("mesh")
    fi = lax.axis_index("freq")

    pairs = (
        (send_hbm, send_ref), (count_hbm, count_ref), (spec_hbm, spec_ref),
        (coords_hbm, coords_ref), (nb_hbm, nb_ref), (inv_hbm, inv_ref), (wind_hbm, wind_ref),
    )
    loads = [pltpu.make_async_copy(a, b, in_sem.at[i]) for i, (a, b) in enumerate(pairs)]
    for load in loads:
        load.start()

    barrier = pltpu.get_barrier_semaphore()
    for off in range(1, n_mesh):
        pl.semaphore_signal(
            barrier, inc=1, device_id={"mesh": lax.rem(me + off, n_mesh)}, device_id_type=MESH
        )

    @pl.when(fi > 0)
    def _():
        pl.semaphore_signal(barrier, inc=1, device_id={"freq": fi - 1}, device_id_type=MESH)

    @pl.when(fi < n_freq - 1)
    def _():
        pl.semaphore_signal(barrier, inc=1, device_id={"freq": fi + 1}, device_id_type=MESH)

    row_id = lax.broadcasted_iota(jnp.int32, (main + tail_rows, LANES), 0)
    direction = jnp.where(row_id < main, row_id, main + (row_id - main) % rest)
    angle = (direction.astype(f32) + 0.5) * (2.0 * math.pi / dirs)
    real = row_id < main + PER * rest
    cosine = jnp.where(real, jnp.cos(angle), 0.0)[:, 0:1]
    sine = jnp.where(real, jnp.sin(angle), 0.0)[:, 0:1]
    ratios = []
    for j in range(band):
        value = jnp.float32(freq_ratio ** (j - NF // 2))
        for b in range(1, n_freq):
            value = jnp.where(fi == b, jnp.float32(freq_ratio ** (b * band + j - NF // 2)), value)
        ratios.append(value)
    speeds = [group_scale / r for r in ratios]

    loads[0].wait()
    cells = send_ref[...].astype(f32)
    lane_c = lax.broadcasted_iota(jnp.int32, (cap, ghosts), 1) % cap
    spread = (lane_c == lax.broadcasted_iota(jnp.int32, (cap, ghosts), 0)).astype(f32)
    wide = jnp.dot(cells, spread, precision=lax.Precision.HIGHEST, preferred_element_type=f32)
    owner_lane = lax.broadcasted_iota(jnp.int32, (n_mesh, ghosts), 1) // cap
    mine = owner_lane == lax.broadcasted_iota(jnp.int32, (n_mesh, ghosts), 0)
    send_row = jnp.sum(jnp.where(mine, wide, 0.0), axis=0, keepdims=True)
    send_row = (send_row + 0.5).astype(jnp.int32)
    lane = lax.broadcasted_iota(jnp.int32, (1, ghosts), 1)
    limit = jnp.zeros((1, ghosts), jnp.int32)
    loads[1].wait()
    for d in range(n_mesh):
        limit = jnp.where(lane // cap == d, count_ref[d], limit)
    send_row = jnp.where(lane % cap < limit, send_row, -1)
    hot_send[...] = (
        (lax.broadcasted_iota(jnp.int32, (nodes, ghosts), 0) == send_row).astype(f32).astype(bf16)
    )

    def copy_of(stage, off, src_rank, dst_rank, target):
        return pltpu.make_async_remote_copy(
            src_ref=pay.at[stage, pl.ds(pl.multiple_of(src_rank * cap, cap), cap), :],
            dst_ref=recv.at[stage, pl.ds(pl.multiple_of(dst_rank * cap, cap), cap), :],
            send_sem=send_sem.at[stage, off],
            recv_sem=recv_sem.at[stage, off],
            device_id={"mesh": target},
            device_id_type=MESH,
        )

    def pack(stage, c):
        both = jnp.dot(lhs[c], hot_send[...], preferred_element_type=f32)
        value = both[:rows] + both[rows:]
        filler = jnp.zeros((LANES - rows, ghosts), f32)
        pay[stage] = jnp.transpose(jnp.concatenate([value, filler], axis=0))

    def send(stage):
        for off in range(1, n_mesh):
            to = lax.rem(me + off, n_mesh)
            copy_of(stage, off, to, me, to).start()

    def own(stage):
        at = pl.ds(pl.multiple_of(me * cap, cap), cap)
        recv[stage, at, :] = pay[stage, at, :]

    def arrive(stage):
        for off in range(1, n_mesh):
            copy_of(stage, off, 0, me, lax.rem(me + off, n_mesh)).wait_recv()

    def ghosts_of(stage):
        hi, lo = split2(jnp.transpose(recv[stage])[:rows])
        return jnp.concatenate([hi, lo], axis=0)

    def split_chunk(c, value):
        hi, lo = split2(value)
        lhs[c, 0:rows] = hi
        lhs[c, rows : 2 * rows] = lo

    loads[2].wait()
    loads[3].wait()
    x_own = coords_ref[0:1, :]
    y_own = coords_ref[1:2, :]
    remains = []
    for row in (x_own, y_own):
        hi, lo = split2(row)
        remains.append((row - hi.astype(f32)) - lo.astype(f32))
    for c in range(chunks):
        parts = [spec_ref[c * PER + j, 0:main, :] for j in range(PER)]
        parts += [spec_ref[c * PER + j, main:dirs, :] for j in range(PER)]
        if c == 0:
            parts += [x_own, y_own] + remains
        else:
            parts += [jnp.zeros((rows - spare, nodes), f32)]
        split_chunk(c, jnp.concatenate(parts, axis=0))
        pack(c, c)

    expected = (n_mesh - 1) + (fi > 0).astype(jnp.int32) + (fi < n_freq - 1).astype(jnp.int32)
    pl.semaphore_wait(barrier, expected)
    for c in range(chunks):
        send(c)

    up_copy = pltpu.make_async_remote_copy(
        src_ref=spec_ref.at[pl.ds(band - REACH, REACH)], dst_ref=halo_lo,
        send_sem=halo_sem.at[0], recv_sem=halo_sem.at[1],
        device_id={"freq": lax.rem(fi + 1, n_freq)}, device_id_type=MESH,
    )
    down_copy = pltpu.make_async_remote_copy(
        src_ref=spec_ref.at[pl.ds(0, UP_REACH)], dst_ref=halo_hi,
        send_sem=halo_sem.at[2], recv_sem=halo_sem.at[3],
        device_id={"freq": lax.rem(fi + n_freq - 1, n_freq)}, device_id_type=MESH,
    )

    @pl.when(fi < n_freq - 1)
    def _():
        up_copy.start()

    @pl.when(fi > 0)
    def _():
        down_copy.start()

    @pl.when(fi == 0)
    def _():
        halo_lo[...] = jnp.zeros(halo_lo.shape, f32)

    @pl.when(fi == n_freq - 1)
    def _():
        halo_hi[...] = jnp.zeros(halo_hi.shape, f32)

    for load in loads[4:]:
        load.wait()
    for c in range(chunks):
        own(c)

    def product(part, k, first, last, side):
        both = jnp.dot(
            part, hot[k, first:last, side * half : (side + 1) * half], preferred_element_type=f32
        )
        return both[:rows] + both[rows:]

    for k in range(slots):
        entry = nb_ref[k : k + 1, :]
        ids = lax.broadcasted_iota(jnp.int32, (nodes + ghosts, nodes), 0)
        hot[k] = (ids == entry).astype(f32).astype(bf16)
    for k in range(slots):
        for c in range(chunks):
            for side in range(2):
                lanes = slice(side * half, (side + 1) * half)
                picked[k, c, :, lanes] = product(lhs[c], k, 0, nodes, side)

    along = cosine[:main] * wind_ref[0:1, :] + sine[:main] * wind_ref[1:2, :]
    along_rest = (
        cosine[main : main + rest] * wind_ref[0:1, :] + sine[main : main + rest] * wind_ref[1:2, :]
    )
    along = jnp.concatenate([along, along_rest], axis=0)

    def sources(j):
        own_bin = spec_ref[j]
        upper = spec_ref[j + UP_REACH] if j + UP_REACH < band else halo_hi[j + UP_REACH - band]
        lower = spec_ref[j - REACH] if j >= REACH else halo_lo[j]
        p1 = roll_rows(upper, -UP_SHIFT)
        m1 = roll_rows(lower, DOWN_SHIFT)
        p2 = roll_rows(upper, UP_SHIFT)
        m2 = roll_rows(lower, -DOWN_SHIFT)
        quad = quad_coupling * (
            own_bin * own_bin * (p1 + m1 + p2 + m2) - 2.0 * own_bin * (p1 * m1 + p2 * m2)
        )
        growth = wind_growth * jnp.maximum(along * ratios[j] - 1.0, 0.0)
        value = own_bin + time_step * (quad + growth * own_bin)
        c, at = divmod(j, PER)
        base[c, at * main : (at + 1) * main, :] = value[:main]
        base[c, tail + at * rest : tail + (at + 1) * rest, :] = value[main:]

    for c in range(chunks):
        base[c, spare:rows, :] = jnp.zeros((rows - spare, nodes), f32)
    middle = range(REACH, band - UP_REACH)
    for j in middle:
        sources(j)

    @pl.when(fi > 0)
    def _():
        up_copy.wait_recv()

    @pl.when(fi < n_freq - 1)
    def _():
        down_copy.wait_recv()

    for j in range(band):
        if j not in middle:
            sources(j)

    scale = time_step * inv_ref[...]
    chunk_row = lax.broadcasted_iota(jnp.int32, (rows, LANES), 0)

    def speed_column(c):
        column = jnp.zeros((rows, LANES), f32)
        for j in range(PER):
            inside = (chunk_row >= j * main) & (chunk_row < (j + 1) * main)
            behind = (chunk_row >= tail + j * rest) & (chunk_row < tail + (j + 1) * rest)
            column = jnp.where(inside | behind, speeds[c * PER + j], column)
        return column[:, 0:1]

    def all_rows(w):
        return jnp.concatenate([w[:main]] * PER + [w[main:]], axis=0)

    def finish(c, lanes, total, column):
        wsum = weights[0, :, lanes]
        for k in range(1, slots):
            wsum = wsum + weights[k, :, lanes]
        return (base[c, :, lanes] + column * total) / (1.0 + column * all_rows(wsum))

    columns = [speed_column(c) for c in range(chunks)]
    for c in range(chunks):
        arrive(c)
        far = ghosts_of(c)
        for side in range(2):
            lanes = slice(side * half, (side + 1) * half)
            total = None
            for k in range(slots):
                value = picked[k, c, :, lanes] + product(far, k, nodes, nodes + ghosts, side)
                if c == 0:
                    dx = value[spare : spare + 1] + value[spare + 2 : spare + 3] - x_own[:, lanes]
                    dy = value[spare + 1 : spare + 2] + value[spare + 3 : spare + 4] - y_own[:, lanes]
                    w = scale[:, lanes] * jnp.maximum(-(cosine * dx + sine * dy), 0.0)
                    weights[k, :, lanes] = w
                else:
                    w = weights[k, :, lanes]
                term = all_rows(w) * value
                total = term if total is None else total + term
            value = finish(c, lanes, total, columns[c])
            hi, lo = split2(value)
            lhs[c, 0:rows, lanes] = hi
            lhs[c, rows : 2 * rows, lanes] = lo
        pack(chunks + c, c)
        send(chunks + c)
        own(chunks + c)
        for side in range(2):
            lanes = slice(side * half, (side + 1) * half)
            total = None
            for k in range(slots):
                term = all_rows(weights[k, :, lanes]) * product(lhs[c], k, 0, nodes, side)
                total = term if total is None else total + term
            acc[c, :, lanes] = total

    for c in range(chunks):
        arrive(chunks + c)
        far = ghosts_of(chunks + c)
        for side in range(2):
            lanes = slice(side * half, (side + 1) * half)
            total = acc[c, :, lanes]
            for k in range(slots):
                total = total + all_rows(weights[k, :, lanes]) * product(
                    far, k, nodes, nodes + ghosts, side
                )
            value = finish(c, lanes, total, columns[c])
            for j in range(PER):
                out_ref[c * PER + j, 0:main, lanes] = value[j * main : (j + 1) * main]
                at = tail + j * rest
                out_ref[c * PER + j, main:dirs, lanes] = value[at : at + rest]

    for stage in range(2 * chunks):
        for off in range(1, n_mesh):
            to = lax.rem(me + off, n_mesh)
            copy_of(stage, off, to, me, to).wait_send()

    @pl.when(fi < n_freq - 1)
    def _():
        up_copy.wait_send()

    @pl.when(fi > 0)
    def _():
        down_copy.wait_send()


def local(n_mesh, n_freq, spectra, coords, inv_area, wind_vector, neighbours, send_nodes, send_count):
    band, dirs, nodes = spectra.shape
    cap = send_nodes.shape[1]
    slots = neighbours.shape[0]
    ghosts = n_mesh * cap
    chunks = band // PER
    main = dirs // 8 * 8
    rows = PER * main + -(-(PER * (dirs - main) + 4) // 8) * 8
    f32, bf16, i32 = jnp.float32, jnp.bfloat16, jnp.int32
    hbm = pl.BlockSpec(memory_space=pltpu.HBM)
    return pl.pallas_call(
        functools.partial(kernel, n_mesh, n_freq, dirs, cap),
        out_shape=jax.ShapeDtypeStruct(spectra.shape, f32),
        in_specs=[hbm] * 7,
        out_specs=pl.BlockSpec(memory_space=pltpu.VMEM),
        scratch_shapes=[
            pltpu.VMEM(spectra.shape, f32),
            pltpu.VMEM(coords.shape, f32),
            pltpu.VMEM((1, nodes), f32),
            pltpu.VMEM(wind_vector.shape, f32),
            pltpu.VMEM(neighbours.shape, i32),
            pltpu.VMEM(send_nodes.shape, i32),
            pltpu.SMEM(send_count.shape, i32),
            pltpu.VMEM((chunks, 2 * rows, nodes), bf16),
            pltpu.VMEM((slots, chunks, rows, nodes), f32),
            pltpu.VMEM((chunks, rows, nodes), f32),
            pltpu.VMEM((chunks, rows, nodes), f32),
            pltpu.VMEM((slots, main + rows - PER * main, nodes), f32),
            pltpu.VMEM((slots, nodes + ghosts, nodes), bf16),
            pltpu.VMEM((nodes, ghosts), bf16),
            pltpu.VMEM((2 * chunks, ghosts, LANES), f32),
            pltpu.VMEM((2 * chunks, ghosts, LANES), f32),
            pltpu.VMEM((REACH, dirs, nodes), f32),
            pltpu.VMEM((UP_REACH, dirs, nodes), f32),
            pltpu.SemaphoreType.DMA((7,)),
            pltpu.SemaphoreType.DMA((2 * chunks, n_mesh)),
            pltpu.SemaphoreType.DMA((2 * chunks, n_mesh)),
            pltpu.SemaphoreType.DMA((4,)),
        ],
        compiler_params=pltpu.CompilerParams(
            collective_id=0, has_side_effects=True, vmem_limit_bytes=64 * 1024 * 1024
        ),
        cost_estimate=pl.CostEstimate(
            flops=4 * 2 * band * dirs * (nodes + ghosts) * nodes * slots,
            bytes_accessed=2 * 4 * band * dirs * nodes,
            transcendentals=0,
        ),
    )(spectra, coords, inv_area.reshape(1, nodes), wind_vector, neighbours, send_nodes, send_count)


def solution(mesh):
    in_specs = (
        P("freq", None, "mesh"),
        P(None, "mesh"),
        P("mesh"),
        P(None, "mesh"),
        P(None, "mesh"),
        P("mesh", None),
        P("mesh"),
    )
    return jax.shard_map(
        functools.partial(local, mesh.shape["mesh"], mesh.shape["freq"]),
        mesh=mesh, in_specs=in_specs, out_specs=P("freq", None, "mesh"), check_vma=False,
    )
```

time: 41.7 us -> 30.1 us (0.72)
  Pallas kernels: 35.2 us -> 27.8 us
  local copies, waits for them, and re-layouts: 6.09 us -> 2.03 us
    pallas_call x1, Pallas kernels: 35.2 us -> 27.8 us  [local(): pl.pallas_call(functools.partial(kernel, n_mesh, n_freq, dirs, cap), out_...]
    unnamed x15 -> x1, local copies, waits for them, and re-layouts: 6.09 us -> 2.03 us
where the time goes in v1:
time: 30.1 us; the launch traced here: 29.9 us
  Pallas kernels  27.8 us (92%)
  local copies, waits for them, and re-layouts  2.03 us (7%)
    pallas_call x1, Pallas kernels, local(): pl.pallas_call(functools.partial(kernel, n_mesh, n_freq, dirs, cap), out_...  27.8 us
    unnamed x1, local copies, waits for them, and re-layouts  2.03 us

profile of v1, /device:TPU:0, one launch (start us, length us, event | category | flops | bytes accessed | tf_op | source)
XLA Modules:
  0.0 29.9 jit_solution(1503967141932833167)
XLA Ops:
  0.0 27.8 %shard_map.73 = f32[9,36,512]{2,1,0:T(8,128)} custom-call(f32[9,36,512]{2,1,0:T(8,128)} %spec_hbm.1, f32[2,512]{1,0:T(2,128)} %coords_hbm.1, f32[1,512]{1,0:T(1,128)} %bitcast.1, f32[2,512]{1,0:T(2,128)} %wind_hbm.1, s32[8,512]{1,0:T(8,128)} %nb_hbm.1, s32[8,32]{1,0:T(8,128)} %send_hbm.1, s32[8]{0:T(128)} %count_hbm.1), custom_call_target="tpu_custom_call" | custom-call | flops 8153726976 | bytes 1327104 | tf_op jit(solution)/shard_map/pallas_call | solution.py:363
  27.9 2.0 %copy.9 = f32[9,36,512]{2,1,0:T(8,128)} copy(f32[9,36,512]{2,1,0:T(8,128)} %shard_map.73) | data formatting | bytes 1327104

commit v2 on v1

--- a/solution.py
+++ b/solution.py
@@ -40,10 +40,10 @@
 def kernel(
     n_mesh, n_freq, dirs, cap,
     spec_hbm, coords_hbm, inv_hbm, wind_hbm, nb_hbm, send_hbm, count_hbm,
-    out_ref,
-    spec_ref, coords_ref, inv_ref, wind_ref, nb_ref, send_ref, count_ref,
+    out_hbm,
+    out_ref, spec_ref, coords_ref, inv_ref, wind_ref, nb_ref, send_ref, count_ref,
     lhs, picked, base, acc, weights, hot, hot_send, pay, recv, halo_lo, halo_hi,
-    in_sem, send_sem, recv_sem, halo_sem,
+    in_sem, send_sem, recv_sem, halo_sem, out_sem,
 ):
     band = spec_ref.shape[0]
     nodes = spec_ref.shape[2]
@@ -57,6 +57,8 @@
     spare = tail + PER * rest
     tail_rows = rows - tail
     half = nodes // 2
+    groups = LANES // cap
+    depth = rows // groups
     f32 = jnp.float32
     bf16 = jnp.bfloat16
     me = lax.axis_index("mesh")
@@ -119,8 +121,8 @@
 
     def copy_of(stage, off, src_rank, dst_rank, target):
         return pltpu.make_async_remote_copy(
-            src_ref=pay.at[stage, pl.ds(pl.multiple_of(src_rank * cap, cap), cap), :],
-            dst_ref=recv.at[stage, pl.ds(pl.multiple_of(dst_rank * cap, cap), cap), :],
+            src_ref=pay.at[stage, src_rank],
+            dst_ref=recv.at[stage, dst_rank],
             send_sem=send_sem.at[stage, off],
             recv_sem=recv_sem.at[stage, off],
             device_id={"mesh": target},
@@ -130,8 +132,11 @@
     def pack(stage, c):
         both = jnp.dot(lhs[c], hot_send[...], preferred_element_type=f32)
         value = both[:rows] + both[rows:]
-        filler = jnp.zeros((LANES - rows, ghosts), f32)
-        pay[stage] = jnp.transpose(jnp.concatenate([value, filler], axis=0))
+        bands = [value[g * depth : (g + 1) * depth] for g in range(groups)]
+        for d in range(n_mesh):
+            pay[stage, d] = jnp.concatenate(
+                [part[:, d * cap : (d + 1) * cap] for part in bands], axis=1
+            )
 
     def send(stage):
         for off in range(1, n_mesh):
@@ -139,15 +144,19 @@
             copy_of(stage, off, to, me, to).start()
 
     def own(stage):
-        at = pl.ds(pl.multiple_of(me * cap, cap), cap)
-        recv[stage, at, :] = pay[stage, at, :]
+        recv[stage, me] = pay[stage, me]
 
     def arrive(stage):
         for off in range(1, n_mesh):
             copy_of(stage, off, 0, me, lax.rem(me + off, n_mesh)).wait_recv()
 
     def ghosts_of(stage):
-        hi, lo = split2(jnp.transpose(recv[stage])[:rows])
+        blocks = [recv[stage, d] for d in range(n_mesh)]
+        bands = [
+            jnp.concatenate([block[:, g * cap : (g + 1) * cap] for block in blocks], axis=1)
+            for g in range(groups)
+        ]
+        hi, lo = split2(jnp.concatenate(bands, axis=0))
         return jnp.concatenate([hi, lo], axis=0)
 
     def split_chunk(c, value):
@@ -172,10 +181,10 @@
             parts += [jnp.zeros((rows - spare, nodes), f32)]
         split_chunk(c, jnp.concatenate(parts, axis=0))
         pack(c, c)
-
-    expected = (n_mesh - 1) + (fi > 0).astype(jnp.int32) + (fi < n_freq - 1).astype(jnp.int32)
-    pl.semaphore_wait(barrier, expected)
-    for c in range(chunks):
+        if c == 0:
+            expected = (n_mesh - 1) + (fi > 0).astype(jnp.int32)
+            expected = expected + (fi < n_freq - 1).astype(jnp.int32)
+            pl.semaphore_wait(barrier, expected)
         send(c)
 
     up_copy = pltpu.make_async_remote_copy(
@@ -320,6 +329,10 @@
                 total = term if total is None else total + term
             acc[c, :, lanes] = total
 
+    def result_of(c):
+        band_of = pl.ds(c * PER, PER)
+        return pltpu.make_async_copy(out_ref.at[band_of], out_hbm.at[band_of], out_sem.at[c])
+
     for c in range(chunks):
         arrive(chunks + c)
         far = ghosts_of(chunks + c)
@@ -335,7 +348,10 @@
                 out_ref[c * PER + j, 0:main, lanes] = value[j * main : (j + 1) * main]
                 at = tail + j * rest
                 out_ref[c * PER + j, main:dirs, lanes] = value[at : at + rest]
-
+        result_of(c).start()
+
+    for c in range(chunks):
+        result_of(c).wait()
     for stage in range(2 * chunks):
         for off in range(1, n_mesh):
             to = lax.rem(me + off, n_mesh)
@@ -364,8 +380,9 @@
         functools.partial(kernel, n_mesh, n_freq, dirs, cap),
         out_shape=jax.ShapeDtypeStruct(spectra.shape, f32),
         in_specs=[hbm] * 7,
-        out_specs=pl.BlockSpec(memory_space=pltpu.VMEM),
+        out_specs=hbm,
         scratch_shapes=[
+            pltpu.VMEM(spectra.shape, f32),
             pltpu.VMEM(spectra.shape, f32),
             pltpu.VMEM(coords.shape, f32),
             pltpu.VMEM((1, nodes), f32),
@@ -380,14 +397,15 @@
             pltpu.VMEM((slots, main + rows - PER * main, nodes), f32),
             pltpu.VMEM((slots, nodes + ghosts, nodes), bf16),
             pltpu.VMEM((nodes, ghosts), bf16),
-            pltpu.VMEM((2 * chunks, ghosts, LANES), f32),
-            pltpu.VMEM((2 * chunks, ghosts, LANES), f32),
+            pltpu.VMEM((2 * chunks, n_mesh, rows * cap // LANES, LANES), f32),
+            pltpu.VMEM((2 * chunks, n_mesh, rows * cap // LANES, LANES), f32),
             pltpu.VMEM((REACH, dirs, nodes), f32),
             pltpu.VMEM((UP_REACH, dirs, nodes), f32),
             pltpu.SemaphoreType.DMA((7,)),
             pltpu.SemaphoreType.DMA((2 * chunks, n_mesh)),
             pltpu.SemaphoreType.DMA((2 * chunks, n_mesh)),
             pltpu.SemaphoreType.DMA((4,)),
+            pltpu.SemaphoreType.DMA((chunks,)),
         ],
         compiler_params=pltpu.CompilerParams(
             collective_id=0, has_side_effects=True, vmem_limit_bytes=64 * 1024 * 1024

time: 30.1 us -> 27 us (0.90)
  Pallas kernels: 27.8 us -> 24.8 us
    pallas_call x1, Pallas kernels: 27.8 us -> 24.8 us  [local(): pl.pallas_call(functools.partial(kernel, n_mesh, n_freq, dirs, cap), out_...]
where the time goes in v2:
time: 27 us; the launch traced here: 26.8 us
  Pallas kernels  24.8 us (92%)
  local copies, waits for them, and re-layouts  2.03 us (8%)
    pallas_call x1, Pallas kernels, local(): pl.pallas_call(functools.partial(kernel, n_mesh, n_freq, dirs, cap), out_...  24.8 us
    unnamed x1, local copies, waits for them, and re-layouts  2.03 us

profile of v2, /device:TPU:0, one launch (start us, length us, event | category | flops | bytes accessed | tf_op | source)
XLA Modules:
  0.0 26.8 jit_solution(11711853950291848907)
XLA Ops:
  0.0 24.8 %shard_map.73 = f32[9,36,512]{2,1,0:T(8,128)} custom-call(f32[9,36,512]{2,1,0:T(8,128)} %spec_hbm.1, f32[2,512]{1,0:T(2,128)} %coords_hbm.1, f32[1,512]{1,0:T(1,128)} %bitcast.1, f32[2,512]{1,0:T(2,128)} %wind_hbm.1, s32[8,512]{1,0:T(8,128)} %nb_hbm.1, s32[8,32]{1,0:T(8,128)} %send_hbm.1, s32[8]{0:T(128)} %count_hbm.1), custom_call_target="tpu_custom_call" | custom-call | flops 8153726976 | bytes 1327104 | tf_op jit(solution)/shard_map/pallas_call | solution.py:379
  24.8 2.0 %copy.9 = f32[9,36,512]{2,1,0:T(8,128)} copy(f32[9,36,512]{2,1,0:T(8,128)} %shard_map.73) | data formatting | bytes 1327104

commit v3 on v2

--- a/solution.py
+++ b/solution.py
@@ -101,14 +101,7 @@
     speeds = [group_scale / r for r in ratios]
 
     loads[0].wait()
-    cells = send_ref[...].astype(f32)
-    lane_c = lax.broadcasted_iota(jnp.int32, (cap, ghosts), 1) % cap
-    spread = (lane_c == lax.broadcasted_iota(jnp.int32, (cap, ghosts), 0)).astype(f32)
-    wide = jnp.dot(cells, spread, precision=lax.Precision.HIGHEST, preferred_element_type=f32)
-    owner_lane = lax.broadcasted_iota(jnp.int32, (n_mesh, ghosts), 1) // cap
-    mine = owner_lane == lax.broadcasted_iota(jnp.int32, (n_mesh, ghosts), 0)
-    send_row = jnp.sum(jnp.where(mine, wide, 0.0), axis=0, keepdims=True)
-    send_row = (send_row + 0.5).astype(jnp.int32)
+    send_row = jnp.concatenate([send_ref[d : d + 1, :] for d in range(n_mesh)], axis=1)
     lane = lax.broadcasted_iota(jnp.int32, (1, ghosts), 1)
     limit = jnp.zeros((1, ghosts), jnp.int32)
     loads[1].wait()
@@ -224,16 +217,6 @@
             part, hot[k, first:last, side * half : (side + 1) * half], preferred_element_type=f32
         )
         return both[:rows] + both[rows:]
-
-    for k in range(slots):
-        entry = nb_ref[k : k + 1, :]
-        ids = lax.broadcasted_iota(jnp.int32, (nodes + ghosts, nodes), 0)
-        hot[k] = (ids == entry).astype(f32).astype(bf16)
-    for k in range(slots):
-        for c in range(chunks):
-            for side in range(2):
-                lanes = slice(side * half, (side + 1) * half)
-                picked[k, c, :, lanes] = product(lhs[c], k, 0, nodes, side)
 
     along = cosine[:main] * wind_ref[0:1, :] + sine[:main] * wind_ref[1:2, :]
     along_rest = (
@@ -260,21 +243,44 @@
 
     for c in range(chunks):
         base[c, spare:rows, :] = jnp.zeros((rows - spare, nodes), f32)
-    middle = range(REACH, band - UP_REACH)
-    for j in middle:
-        sources(j)
-
-    @pl.when(fi > 0)
-    def _():
-        up_copy.wait_recv()
-
-    @pl.when(fi < n_freq - 1)
-    def _():
-        down_copy.wait_recv()
-
-    for j in range(band):
-        if j not in middle:
-            sources(j)
+
+    def hot_columns(k):
+        entry = nb_ref[k : k + 1, :]
+        ids = lax.broadcasted_iota(jnp.int32, (nodes + ghosts, nodes), 0)
+        hot[k] = (ids == entry).astype(f32).astype(bf16)
+
+    def pick_local(k):
+        every = lhs[...].reshape(chunks * 2 * rows, nodes)
+        for side in range(2):
+            lanes = slice(side * half, (side + 1) * half)
+            both = jnp.dot(every, hot[k, 0:nodes, lanes], preferred_element_type=f32)
+            for c in range(chunks):
+                at = c * 2 * rows
+                picked[k, c, :, lanes] = both[at : at + rows] + both[at + rows : at + 2 * rows]
+
+    middle = list(range(REACH, band - UP_REACH))
+    outer = [j for j in range(band) if j not in middle]
+    first = slots // 2
+    hot_columns(0)
+    for k in range(slots):
+        if k == first:
+            @pl.when(fi > 0)
+            def _():
+                up_copy.wait_recv()
+
+            @pl.when(fi < n_freq - 1)
+            def _():
+                down_copy.wait_recv()
+
+        if k + 1 < slots:
+            hot_columns(k + 1)
+        pick_local(k)
+        if k < first:
+            for j in middle[k::first]:
+                sources(j)
+        else:
+            for j in outer[k - first :: slots - first]:
+                sources(j)
 
     scale = time_step * inv_ref[...]
     chunk_row = lax.broadcasted_iota(jnp.int32, (rows, LANES), 0)

time: 27 us -> 27 us (level)
  no operation moved by 1% of the time
where the time goes in v3:
time: 27 us; the launch traced here: 26.8 us
  Pallas kernels  24.8 us (92%)
  local copies, waits for them, and re-layouts  2.03 us (8%)
    pallas_call x1, Pallas kernels, local(): pl.pallas_call(functools.partial(kernel, n_mesh, n_freq, dirs, cap), out_...  24.8 us
    unnamed x1, local copies, waits for them, and re-layouts  2.03 us

profile of v3, /device:TPU:0, one launch (start us, length us, event | category | flops | bytes accessed | tf_op | source)
XLA Modules:
  0.0 26.8 jit_solution(18078561441842850710)
XLA Ops:
  0.0 24.8 %shard_map.73 = f32[9,36,512]{2,1,0:T(8,128)} custom-call(f32[9,36,512]{2,1,0:T(8,128)} %spec_hbm.1, f32[2,512]{1,0:T(2,128)} %coords_hbm.1, f32[1,512]{1,0:T(1,128)} %bitcast.1, f32[2,512]{1,0:T(2,128)} %wind_hbm.1, s32[8,512]{1,0:T(8,128)} %nb_hbm.1, s32[8,32]{1,0:T(8,128)} %send_hbm.1, s32[8]{0:T(128)} %count_hbm.1), custom_call_target="tpu_custom_call" | custom-call | flops 8153726976 | bytes 1327104 | tf_op jit(solution)/shard_map/pallas_call | solution.py:385
  24.8 2.0 %copy.9 = f32[9,36,512]{2,1,0:T(8,128)} copy(f32[9,36,512]{2,1,0:T(8,128)} %shard_map.73) | data formatting | bytes 1327104

commit v4 on v3

--- a/solution.py
+++ b/solution.py
@@ -42,7 +42,7 @@
     spec_hbm, coords_hbm, inv_hbm, wind_hbm, nb_hbm, send_hbm, count_hbm,
     out_hbm,
     out_ref, spec_ref, coords_ref, inv_ref, wind_ref, nb_ref, send_ref, count_ref,
-    lhs, picked, base, acc, weights, hot, hot_send, pay, recv, halo_lo, halo_hi,
+    lhs, picked, base, acc, shares, weights, hot, hot_send, pay, recv, halo_lo, halo_hi,
     in_sem, send_sem, recv_sem, halo_sem, out_sem,
 ):
     band = spec_ref.shape[0]
@@ -296,11 +296,11 @@
     def all_rows(w):
         return jnp.concatenate([w[:main]] * PER + [w[main:]], axis=0)
 
-    def finish(c, lanes, total, column):
+    def divisor(lanes, column):
         wsum = weights[0, :, lanes]
         for k in range(1, slots):
             wsum = wsum + weights[k, :, lanes]
-        return (base[c, :, lanes] + column * total) / (1.0 + column * all_rows(wsum))
+        return 1.0 / (1.0 + column * all_rows(wsum))
 
     columns = [speed_column(c) for c in range(chunks)]
     for c in range(chunks):
@@ -320,36 +320,51 @@
                     w = weights[k, :, lanes]
                 term = all_rows(w) * value
                 total = term if total is None else total + term
-            value = finish(c, lanes, total, columns[c])
+            share = divisor(lanes, columns[c])
+            value = (base[c, :, lanes] + columns[c] * total) * share
+            shares[c, :, lanes] = share
             hi, lo = split2(value)
             lhs[c, 0:rows, lanes] = hi
             lhs[c, rows : 2 * rows, lanes] = lo
         pack(chunks + c, c)
         send(chunks + c)
         own(chunks + c)
+
+    for side in range(2):
+        lanes = slice(side * half, (side + 1) * half)
+        for k in range(slots):
+            every = lhs[...].reshape(chunks * 2 * rows, nodes)
+            both = jnp.dot(every, hot[k, 0:nodes, lanes], preferred_element_type=f32)
+            w = all_rows(weights[k, :, lanes])
+            for c in range(chunks):
+                at = c * 2 * rows
+                term = w * (both[at : at + rows] + both[at + rows : at + 2 * rows])
+                if k == 0:
+                    acc[c, :, lanes] = term
+                elif k < slots - 1:
+                    acc[c, :, lanes] += term
+                else:
+                    share = shares[c, :, lanes]
+                    total = acc[c, :, lanes] + term
+                    acc[c, :, lanes] = (base[c, :, lanes] + columns[c] * total) * share
+                    shares[c, :, lanes] = columns[c] * share
+
+    def result_of(c):
+        band_of = pl.ds(c * PER, PER)
+        return pltpu.make_async_copy(out_ref.at[band_of], out_hbm.at[band_of], out_sem.at[c])
+
+    for c in range(chunks):
+        arrive(chunks + c)
+        far = ghosts_of(chunks + c)
         for side in range(2):
             lanes = slice(side * half, (side + 1) * half)
             total = None
             for k in range(slots):
-                term = all_rows(weights[k, :, lanes]) * product(lhs[c], k, 0, nodes, side)
-                total = term if total is None else total + term
-            acc[c, :, lanes] = total
-
-    def result_of(c):
-        band_of = pl.ds(c * PER, PER)
-        return pltpu.make_async_copy(out_ref.at[band_of], out_hbm.at[band_of], out_sem.at[c])
-
-    for c in range(chunks):
-        arrive(chunks + c)
-        far = ghosts_of(chunks + c)
-        for side in range(2):
-            lanes = slice(side * half, (side + 1) * half)
-            total = acc[c, :, lanes]
-            for k in range(slots):
-                total = total + all_rows(weights[k, :, lanes]) * product(
+                term = all_rows(weights[k, :, lanes]) * product(
                     far, k, nodes, nodes + ghosts, side
                 )
-            value = finish(c, lanes, total, columns[c])
+                total = term if total is None else total + term
+            value = acc[c, :, lanes] + shares[c, :, lanes] * total
             for j in range(PER):
                 out_ref[c * PER + j, 0:main, lanes] = value[j * main : (j + 1) * main]
                 at = tail + j * rest
@@ -370,6 +385,17 @@
     @pl.when(fi > 0)
     def _():
         down_copy.wait_send()
+
+
+def hand_over(swept, result, sem):
+    band = swept.shape[0]
+    copies = [
+        pltpu.make_async_copy(swept.at[j], result.at[j], sem.at[j]) for j in range(band)
+    ]
+    for copy in copies:
+        copy.start()
+    for copy in copies:
+        copy.wait()
 
 
 def local(n_mesh, n_freq, spectra, coords, inv_area, wind_vector, neighbours, send_nodes, send_count):
@@ -382,7 +408,7 @@
     rows = PER * main + -(-(PER * (dirs - main) + 4) // 8) * 8
     f32, bf16, i32 = jnp.float32, jnp.bfloat16, jnp.int32
     hbm = pl.BlockSpec(memory_space=pltpu.HBM)
-    return pl.pallas_call(
+    swept = pl.pallas_call(
         functools.partial(kernel, n_mesh, n_freq, dirs, cap),
         out_shape=jax.ShapeDtypeStruct(spectra.shape, f32),
         in_specs=[hbm] * 7,
@@ -398,6 +424,7 @@
             pltpu.SMEM(send_count.shape, i32),
             pltpu.VMEM((chunks, 2 * rows, nodes), bf16),
             pltpu.VMEM((slots, chunks, rows, nodes), f32),
+            pltpu.VMEM((chunks, rows, nodes), f32),
             pltpu.VMEM((chunks, rows, nodes), f32),
             pltpu.VMEM((chunks, rows, nodes), f32),
             pltpu.VMEM((slots, main + rows - PER * main, nodes), f32),
@@ -422,6 +449,14 @@
             transcendentals=0,
         ),
     )(spectra, coords, inv_area.reshape(1, nodes), wind_vector, neighbours, send_nodes, send_count)
+    return pl.pallas_call(
+        hand_over,
+        out_shape=jax.ShapeDtypeStruct(spectra.shape, f32),
+        in_specs=[hbm],
+        out_specs=hbm,
+        scratch_shapes=[pltpu.SemaphoreType.DMA((band,))],
+        compiler_params=pltpu.CompilerParams(vmem_limit_bytes=64 * 1024 * 1024),
+    )(swept)
 
 
 def solution(mesh):

time: 27 us -> 48.9 us (1.81)
  Pallas kernels: 24.8 us -> 48.7 us
  local copies, waits for them, and re-layouts: 2.03 us -> 0 us
    pallas_call x0 -> x1, Pallas kernels: none -> 23.5 us  [local(): pl.pallas_call(hand_over, out_shape=jax.ShapeDtypeStruct(spectra.shape, f...]
    unnamed x1 -> x0, local copies, waits for them, and re-layouts: 2.03 us -> none
where the time goes in v4:
time: 48.9 us; the launch traced here: 48.7 us
  Pallas kernels  48.7 us (100%)
    pallas_call x1, Pallas kernels, local(): pl.pallas_call(functools.partial(kernel, n_mesh, n_freq, dirs, cap), out_...  25.2 us
    pallas_call x1, Pallas kernels, local(): pl.pallas_call(hand_over, out_shape=jax.ShapeDtypeStruct(spectra.shape, f...  23.5 us

profile of v4, /device:TPU:0, one launch (start us, length us, event | category | flops | bytes accessed | tf_op | source)
XLA Modules:
  0.0 48.7 jit_solution(587452840624643037)
XLA Ops:
  0.0 25.2 %shard_map.73.swept = f32[9,36,512]{2,1,0:T(8,128)} custom-call(f32[9,36,512]{2,1,0:T(8,128)} %spec_hbm.1, f32[2,512]{1,0:T(2,128)} %coords_hbm.1, f32[1,512]{1,0:T(1,128)} %bitcast.1, f32[2,512]{1,0:T(2,128)} %wind_hbm.1, s32[8,512]{1,0:T(8,128)} %nb_hbm.1, s32[8,32]{1,0:T(8,128)} %send_hbm.1, s32[8]{0:T(128)} %count_hbm.1), custom_call_target="tpu_custom_call" | custom-call | flops 8153726976 | bytes 1327104 | tf_op jit(solution)/shard_map/pallas_call | solution.py:411
  25.2 23.5 %shard_map.74 = f32[9,36,512]{2,1,0:T(8,128)} custom-call(f32[9,36,512]{2,1,0:T(8,128)} %shard_map.73.swept), custom_call_target="tpu_custom_call" | custom-call | tf_op jit(solution)/shard_map/pallas_call | solution.py:452

commit v5 on v4

--- a/solution.py
+++ b/solution.py
@@ -139,6 +139,11 @@
     def own(stage):
         recv[stage, me] = pay[stage, me]
 
+    def leave(stage):
+        for off in range(1, n_mesh):
+            to = lax.rem(me + off, n_mesh)
+            copy_of(stage, off, to, me, to).wait_send()
+
     def arrive(stage):
         for off in range(1, n_mesh):
             copy_of(stage, off, 0, me, lax.rem(me + off, n_mesh)).wait_recv()
@@ -178,7 +183,8 @@
             expected = (n_mesh - 1) + (fi > 0).astype(jnp.int32)
             expected = expected + (fi < n_freq - 1).astype(jnp.int32)
             pl.semaphore_wait(barrier, expected)
-        send(c)
+        if c < chunks - 1:
+            send(c)
 
     up_copy = pltpu.make_async_remote_copy(
         src_ref=spec_ref.at[pl.ds(band - REACH, REACH)], dst_ref=halo_lo,
@@ -272,6 +278,9 @@
             def _():
                 down_copy.wait_recv()
 
+        if k == slots - 2:
+            leave(0)
+            send(chunks - 1)
         if k + 1 < slots:
             hot_columns(k + 1)
         pick_local(k)
@@ -373,10 +382,8 @@
 
     for c in range(chunks):
         result_of(c).wait()
-    for stage in range(2 * chunks):
-        for off in range(1, n_mesh):
-            to = lax.rem(me + off, n_mesh)
-            copy_of(stage, off, to, me, to).wait_send()
+    for stage in range(1, 2 * chunks):
+        leave(stage)
 
     @pl.when(fi < n_freq - 1)
     def _():
@@ -387,15 +394,21 @@
         down_copy.wait_send()
 
 
-def hand_over(swept, result, sem):
-    band = swept.shape[0]
-    copies = [
-        pltpu.make_async_copy(swept.at[j], result.at[j], sem.at[j]) for j in range(band)
+def hand_over(swept, result, held, in_sem, out_sem):
+    parts = [pl.ds(j, PER) for j in range(0, swept.shape[0], PER)]
+    loads = [
+        pltpu.make_async_copy(swept.at[p], held.at[p], in_sem.at[i]) for i, p in enumerate(parts)
     ]
-    for copy in copies:
-        copy.start()
-    for copy in copies:
-        copy.wait()
+    stores = [
+        pltpu.make_async_copy(held.at[p], result.at[p], out_sem.at[i]) for i, p in enumerate(parts)
+    ]
+    for load in loads:
+        load.start()
+    for load, store in zip(loads, stores):
+        load.wait()
+        store.start()
+    for store in stores:
+        store.wait()
 
 
 def local(n_mesh, n_freq, spectra, coords, inv_area, wind_vector, neighbours, send_nodes, send_count):
@@ -454,7 +467,11 @@
         out_shape=jax.ShapeDtypeStruct(spectra.shape, f32),
         in_specs=[hbm],
         out_specs=hbm,
-        scratch_shapes=[pltpu.SemaphoreType.DMA((band,))],
+        scratch_shapes=[
+            pltpu.VMEM(spectra.shape, f32),
+            pltpu.SemaphoreType.DMA((chunks,)),
+            pltpu.SemaphoreType.DMA((chunks,)),
+        ],
         compiler_params=pltpu.CompilerParams(vmem_limit_bytes=64 * 1024 * 1024),
     )(swept)
 

time: 48.9 us -> 27 us (0.55)
  the two profiles are of different devices: /device:TPU:0 before, /device:TPU:1 now
where the time goes in v5:
time: 27 us; the launch traced here: 26.8 us
  Pallas kernels  26.8 us (99%)
    pallas_call x1, Pallas kernels, local(): pl.pallas_call(functools.partial(kernel, n_mesh, n_freq, dirs, cap), out_...  24.9 us
    pallas_call x1, Pallas kernels, local(): pl.pallas_call(hand_over, out_shape=jax.ShapeDtypeStruct(spectra.shape, f...  1.93 us

profile of v5, /device:TPU:1, one launch (start us, length us, event | category | flops | bytes accessed | tf_op | source)
XLA Modules:
  0.0 26.8 jit_solution(5981567417301274066)
XLA Ops:
  0.0 24.9 %shard_map.73.swept = f32[9,36,512]{2,1,0:T(8,128)} custom-call(f32[9,36,512]{2,1,0:T(8,128)} %spec_hbm.1, f32[2,512]{1,0:T(2,128)} %coords_hbm.1, f32[1,512]{1,0:T(1,128)} %bitcast.1, f32[2,512]{1,0:T(2,128)} %wind_hbm.1, s32[8,512]{1,0:T(8,128)} %nb_hbm.1, s32[8,32]{1,0:T(8,128)} %send_hbm.1, s32[8]{0:T(128)} %count_hbm.1), custom_call_target="tpu_custom_call" | custom-call | flops 8153726976 | bytes 1327104 | tf_op jit(solution)/shard_map/pallas_call | solution.py:424
  24.9 1.9 %shard_map.74 = f32[9,36,512]{2,1,0:T(8,128)} custom-call(f32[9,36,512]{2,1,0:T(8,128)} %shard_map.73.swept), custom_call_target="tpu_custom_call" | custom-call | tf_op jit(solution)/shard_map/pallas_call | solution.py:465
